TPU v7x, 32 devices: a whole 2x2x4 slice. The times are simulated.
32 devices in a mesh: groups: 2 (over x), replica: 2 (over core), tensor: 8 (over z, y).
Axes of the slice: x: 2, y: 2, z: 4, core: 2. Of those that a mesh axis runs over, the one named last changes fastest.
Arguments:
- hidden: bfloat16 [128, 8192], P(('groups', 'replica'), 'tensor'), parts along dimension 0, may hold values from -6 to 6
- w_query: bfloat16 [8192, 8192], P(None, 'tensor'), may hold values from -0.0625 to 0.0625
- output_weight: bfloat16 [8192, 8192], P('tensor'), may hold values from -0.09375 to 0.09375
- keys: bfloat16 [128, 8, 32, 128], P(('groups', 'replica')), parts along dimension 0
- values: bfloat16 [128, 8, 32, 128], P(('groups', 'replica')), parts along dimension 0, may hold values from -6 to 6
- query_down_maps: bfloat16 [16, 64, 8192], P(('groups', 'replica'), None, 'tensor'), parts along dimension 0, may hold values from -0.0625 to 0.0625
- query_up_maps: bfloat16 [16, 64, 8192], P(('groups', 'replica'), None, 'tensor'), parts along dimension 0, may hold values from -0.75 to 0.75
- output_down_maps: bfloat16 [16, 64, 8192], P(('groups', 'replica'), None, 'tensor'), parts along dimension 0, may hold values from -0.0625 to 0.0625
- output_up_maps: bfloat16 [16, 64, 8192], P(('groups', 'replica'), None, 'tensor'), parts along dimension 0, may hold values from -0.75 to 0.75
- adapter_ids: int32 [128], P('groups'), parts along dimension 0, may hold values from 0 to 7
- owner_map: int32 [16], P('groups'), parts along dimension 0, may hold values from 0 to 7, each once
- kv_lengths: int32 [128], P(('groups', 'replica')), parts along dimension 0, may hold values from 1 to 32, as said below
Outputs:
- attn_out: bfloat16 [128, 8192], P(('groups', 'replica'), 'tensor'), parts along dimension 0
There are 2 independent parts, one for each index of `groups`. A program takes and returns all parts, laid end to end along the dimension named above; an argument that names none is the same for every part. Nothing has to cross between parts.
Inputs may be any that keep to these rules, and one draw needn't show every extreme that they name: `owner_map`: every request's adapter has a slot; slot s is stored at replica index s // 4. Request r attends to its first kv_lengths[r] cached positions; some request holds all 32.
All inputs are finite; a program needn't handle non-finite values.
Results may differ from a plain program's by a relative error of at most 0.0092.
Values may be sent and summed in bfloat16 or wider, within the bound.
A program may use at most 128 MiB of HBM per device.

v0:
```python
import functools
import math

import jax
import jax.numpy as jnp
from jax import lax
from jax.experimental import pallas as pl
from jax.experimental.pallas import tpu as pltpu
from jax.sharding import PartitionSpec as P

HEADS = 64
KVS = 8
ROW_BLOCK = 8
F32 = jnp.float32
BF16 = jnp.bfloat16


def loop(count, body, first=0):
    def step(k, carry):
        body(k)
        return carry

    if count > first:
        lax.fori_loop(first, count, step, 0)


def remote(src, dst, send_sem, recv_sem, device):
    return pltpu.make_async_remote_copy(
        src_ref=src,
        dst_ref=dst,
        send_sem=send_sem,
        recv_sem=recv_sem,
        device_id=device,
        device_id_type=pl.DeviceIdType.MESH,
    )


def block_kernel(
    tensor,
    replicas,
    hidden,
    w_query,
    output_weight,
    keys,
    values,
    query_down,
    query_up,
    output_down,
    output_up,
    ids,
    owners,
    lengths,
    out,
    h_buf,
    wq_buf,
    ow_buf,
    key_buf,
    value_buf,
    map_buf,
    acc,
    mixed,
    low_send,
    low_recv,
    pair_send,
    pair_recv,
    far_send,
    far_recv,
    h_local,
    wq_sem,
    ow_sem,
    kv_sem,
    map_local,
    map_send_sem,
    map_recv_sem,
    h_send_sem,
    h_recv_sem,
    fwd_send_sem,
    low_send_sem,
    low_recv_sem,
    pair_send_sem,
    pair_recv_sem,
    far_send_sem,
    far_recv_sem,
):
    rows, width = hidden.shape
    cols = w_query.shape[1]
    head_size = keys.shape[3]
    length = keys.shape[2]
    stored, rank, _ = query_down.shape
    adapters = stored * replicas
    lanes = low_send.shape[2]
    packed = lanes // rank
    inner = 2 if tensor % 2 == 0 else 1
    outer = tensor // inner
    me = lax.axis_index("tensor")
    rep = lax.axis_index("replica")
    o, i = me // inner, me % inner

    def at(k, j):
        return ((o + k) % outer) * inner + (i + j) % inner

    barrier = pltpu.get_barrier_semaphore()
    for k in range(1, tensor):
        pl.semaphore_signal(
            barrier, inc=1, device_id={"tensor": (me + k) % tensor}, device_id_type=pl.DeviceIdType.MESH
        )
    for k in range(1, replicas):
        pl.semaphore_signal(
            barrier, inc=1, device_id={"replica": (rep + k) % replicas}, device_id_type=pl.DeviceIdType.MESH
        )

    own_hidden = pltpu.make_async_copy(hidden, h_buf.at[me], h_local)
    own_hidden.start()
    maps = (query_down, query_up, output_down, output_up)
    own_slots = pl.ds(pl.multiple_of(rep * stored, stored), stored)
    own_maps = [
        pltpu.make_async_copy(maps[m], map_buf.at[m, own_slots], map_local.at[m]) for m in range(4)
    ]

    def shard(n):
        return ((o + outer - n % outer) % outer) * inner + (i + n // outer) % inner

    def target(n):
        return at((n + 1) % outer, inner - 1 - n // outer)

    def wq_copy(s):
        return pltpu.make_async_copy(
            w_query.at[pl.ds(pl.multiple_of(s * width, width), width), :], wq_buf.at[s], wq_sem.at[s]
        )

    def ow_copy(s):
        return pltpu.make_async_copy(
            output_weight.at[:, pl.ds(pl.multiple_of(s * width, width), width)], ow_buf.at[s], ow_sem.at[s]
        )

    own_maps[0].start()
    local_heads = cols // head_size
    group = HEADS // KVS
    kv_count = max(1, local_heads // group)
    first_kv = me * local_heads // group
    kv_copies = []
    for j in range(kv_count):
        kv_copies.append(pltpu.make_async_copy(keys.at[:, first_kv + j], key_buf.at[j], kv_sem.at[0, j]))
        kv_copies.append(pltpu.make_async_copy(values.at[:, first_kv + j], value_buf.at[j], kv_sem.at[1, j]))
    ahead = min(4, tensor)
    for n in range(ahead):
        wq_copy(shard(n)).start()

    pl.semaphore_wait(barrier, tensor - 1 + replicas - 1)
    own_hidden.wait()

    h_sends = []
    for k in range(1, outer):
        h_sends.append(
            remote(
                h_buf.at[me], h_buf.at[me], h_send_sem.at[k], h_recv_sem.at[me], {"tensor": at(k, 0)}
            )
        )
    if inner == 2:
        h_sends.append(
            remote(h_buf.at[me], h_buf.at[me], h_send_sem.at[0], h_recv_sem.at[me], {"tensor": at(0, 1)})
        )
    for copy in h_sends:
        copy.start()

    map_copies = []

    def send_map(m):
        for k in range(1, replicas):
            map_copies.append(
                remote(
                    maps[m],
                    map_buf.at[m, own_slots],
                    map_send_sem.at[m, k],
                    map_recv_sem.at[m, rep],
                    {"replica": (rep + k) % replicas},
                )
            )
            map_copies[-1].start()

    send_map(0)
    send_map(1)
    own_maps[1].start()
    for copy in kv_copies:
        copy.start()

    def wait_map(m):
        own_maps[m].wait()
        for k in range(1, replicas):
            other = (rep + k) % replicas
            block = map_buf.at[m, pl.ds(pl.multiple_of(other * stored, stored), stored)]
            remote(block, block, map_send_sem.at[m, k], map_recv_sem.at[m, other], {"replica": other}).wait_recv()

    def down_rows(line, first):
        size = line.shape[1]
        row = lax.broadcasted_iota(jnp.int32, (rows, size), 0) + first
        column = lax.broadcasted_iota(jnp.int32, (rows, size), 1)
        return jnp.sum(jnp.where(row == column, line.astype(F32), 0.0), axis=1, keepdims=True)

    own_ids = down_rows(ids[...], rep * rows)
    held = down_rows(lengths[...], 0)
    table = lax.broadcasted_iota(jnp.int32, (rows, owners.shape[1]), 1).astype(F32)
    slot = jnp.sum(jnp.where(own_ids == table, owners[...].astype(F32), 0.0), axis=1, keepdims=True)
    lane = lax.broadcasted_iota(jnp.int32, (rows, adapters * rank), 1) // rank
    pick = lane.astype(F32) == slot
    lower = lax.broadcasted_iota(jnp.int32, (rows // packed, lanes), 1) < rank

    def turned(x):
        return jnp.concatenate([x[:, rank:], x[:, :rank]], axis=1)

    def send_low(which, features):
        down = map_buf[2 * which].reshape(adapters * rank, width)
        part = lax.dot_general(features, down, (((1,), (1,)), ((), ())), preferred_element_type=F32)
        part = jnp.where(pick, part, 0.0)
        part = sum(part[:, c : c + lanes] for c in range(0, adapters * rank, lanes))
        if packed == 2:
            part = part + turned(part)
            part = jnp.where(lower, part[: rows // 2], part[rows // 2 :])
        low_send[which] = part
        copies = []
        for k in range(1, tensor):
            copies.append(
                remote(
                    low_send.at[which],
                    low_recv.at[which, me],
                    low_send_sem.at[which, k],
                    low_recv_sem.at[which, me],
                    {"tensor": (me + k) % tensor},
                )
            )
            copies[-1].start()
        return copies

    def adapter_delta(which):
        total = low_send[which]
        for k in range(1, tensor):
            s = (me + k) % tensor
            remote(
                low_send.at[which], low_recv.at[which, s], low_send_sem.at[which, k], low_recv_sem.at[which, s], {"tensor": s}
            ).wait_recv()
            total = total + low_recv[which, s]
        if packed == 2:
            other = turned(total)
            total = jnp.concatenate(
                [jnp.where(lower, total, other), jnp.where(lower, other, total)], axis=0
            )
        spread = jnp.concatenate([total] * (adapters * rank // lanes), axis=1)
        spread = jnp.where(pick, spread, 0.0).astype(BF16)
        up = map_buf[2 * which + 1].reshape(adapters * rank, width)
        return 0.5 * jnp.dot(spread, up, preferred_element_type=F32)

    def wait_hidden(s):
        remote(h_buf.at[s], h_buf.at[s], h_send_sem.at[0], h_recv_sem.at[s], {"tensor": at(0, 1)}).wait_recv()

    acc[...] = jnp.zeros_like(acc)

    def forward(n):
        s = shard(n)
        return remote(h_buf.at[s], h_buf.at[s], fwd_send_sem.at[n], h_recv_sem.at[s], {"tensor": at(0, 1)})

    def use_shard(n):
        following = shard(n + 1)

        @pl.when(n + 1 < tensor)
        def _():
            wait_hidden(following)

        if inner == 2:

            @pl.when(n + 1 < outer)
            def _():
                forward(n + 1).start()

        @pl.when(n + ahead < tensor)
        def _():
            wq_copy(shard(n + ahead)).start()

        ow_copy(target(n)).start()
        s = shard(n)
        wq_copy(s).wait()
        acc[...] += jnp.dot(h_buf[s], wq_buf[s], preferred_element_type=F32)

    first, second = tensor * 3 // 8, tensor * 7 // 8
    loop(first, use_shard)
    wait_map(0)
    low_copies = send_low(0, h_buf[me])
    loop(second, use_shard, first)
    wait_map(1)
    acc[...] += adapter_delta(0)
    loop(tensor, use_shard, second)
    for m in range(2, 4):
        send_map(m)
        own_maps[m].start()
    query = acc[...]

    for copy in kv_copies:
        copy.wait()
    per_kv = local_heads // kv_count
    shape = (per_kv * ROW_BLOCK, ROW_BLOCK * length)
    row = lax.broadcasted_iota(jnp.int32, shape, 0) % ROW_BLOCK
    column = lax.broadcasted_iota(jnp.int32, shape, 1)
    position = (column - row * length).astype(F32)
    for j in range(kv_count):
        for b in range(0, rows, ROW_BLOCK):
            heads = [
                query[b : b + ROW_BLOCK, h * head_size : (h + 1) * head_size]
                for h in range(j * per_kv, (j + 1) * per_kv)
            ]
            q = jnp.concatenate(heads, axis=0).astype(BF16)
            key = key_buf[j, b : b + ROW_BLOCK].reshape(ROW_BLOCK * length, head_size)
            value = value_buf[j, b : b + ROW_BLOCK].reshape(ROW_BLOCK * length, head_size)
            live = jnp.concatenate([held[b : b + ROW_BLOCK]] * per_kv, axis=0)
            scores = lax.dot_general(q, key, (((1,), (1,)), ((), ())), preferred_element_type=F32)
            scores = scores * (1.0 / math.sqrt(head_size))
            scores = jnp.where((position >= 0) & (position < live), scores, -1e30)
            top = jnp.max(scores, axis=1, keepdims=True)
            weights = jnp.exp(scores - top)
            probs = (weights / jnp.sum(weights, axis=1, keepdims=True)).astype(BF16)
            result = jnp.dot(probs, value, preferred_element_type=F32)
            for n in range(per_kv):
                h = j * per_kv + n
                mixed[b : b + ROW_BLOCK, h * head_size : (h + 1) * head_size] = result[
                    n * ROW_BLOCK : (n + 1) * ROW_BLOCK
                ]

    features = mixed[...].astype(BF16)
    def pair_copy(k):
        d = (o + k) % outer
        return remote(
            pair_send.at[k], pair_recv.at[d], pair_send_sem.at[k], pair_recv_sem.at[d], {"tensor": at(0, 1)}
        )

    def far_copy(k):
        return remote(far_send.at[k], far_recv.at[o], far_send_sem.at[k], far_recv_sem.at[o], {"tensor": at(k, 0)})

    def product(s):
        ow_copy(s).wait()
        return jnp.dot(features, ow_buf[s], preferred_element_type=F32)

    def to_pair(n):
        k = (n + 1) % outer
        pair_send[k] = product(at(k, 1)).astype(BF16)
        pair_copy(k).start()

    early = outer // 2 if inner == 2 else 0
    loop(early, to_pair)
    wait_map(2)
    low_copies += send_low(1, features)
    if inner == 2:
        loop(outer, to_pair, early)

    def own_sum(k):
        total = product(at(k, 0))
        if inner == 2:
            pair_copy(k).wait_recv()
            total = total + pair_recv[(o + k) % outer].astype(F32)
        return total

    def to_far(k):
        far_send[k] = own_sum(k).astype(BF16)
        far_copy(k).start()

    loop(outer, to_far, 1)
    wait_map(3)
    total = adapter_delta(1)
    total = total + own_sum(0)
    for k in range(1, outer):
        s = (o + k) % outer
        remote(far_send.at[k], far_recv.at[s], far_send_sem.at[k], far_recv_sem.at[s], {"tensor": at(k, 0)}).wait_recv()
        total = total + far_recv[s].astype(F32)
    out[...] = total.astype(BF16)

    for copy in h_sends + map_copies + low_copies:
        copy.wait_send()
    for k in range(outer):
        if k > 0:
            far_copy(k).wait_send()
        if inner == 2:
            pair_copy(k).wait_send()
            if k > 0:
                forward(k).wait_send()


def per_device(tensor, replicas, *args):
    (
        hidden,
        w_query,
        output_weight,
        keys,
        values,
        query_down,
        query_up,
        output_down,
        output_up,
        adapter_ids,
        owner_map,
        kv_lengths,
    ) = args
    rows, width = hidden.shape
    cols = w_query.shape[1]
    stored, rank, _ = query_down.shape
    length, head_size = keys.shape[2:]
    kv_count = max(1, cols // head_size // (HEADS // KVS))
    inner = 2 if tensor % 2 == 0 else 1
    outer = tensor // inner
    lanes = max(128, rank)
    dma = pltpu.SemaphoreType.DMA
    any_spec = pl.BlockSpec(memory_space=pl.ANY)
    vmem_spec = pl.BlockSpec(memory_space=pltpu.VMEM)
    return pl.pallas_call(
        functools.partial(block_kernel, tensor, replicas),
        out_shape=pltpu.VMEM((rows, width), BF16),
        in_specs=[any_spec] * 9 + [vmem_spec] * 3,
        out_specs=vmem_spec,
        scratch_shapes=[
            pltpu.VMEM((tensor, rows, width), BF16),
            pltpu.VMEM((tensor, width, cols), BF16),
            pltpu.VMEM((tensor, cols, width), BF16),
            pltpu.VMEM((kv_count, rows, length, head_size), BF16),
            pltpu.VMEM((kv_count, rows, length, head_size), BF16),
            pltpu.VMEM((4, replicas * stored, rank, width), BF16),
            pltpu.VMEM((rows, cols), F32),
            pltpu.VMEM((rows, cols), F32),
            pltpu.VMEM((2, rows * rank // lanes, lanes), F32),
            pltpu.VMEM((2, tensor, rows * rank // lanes, lanes), F32),
            pltpu.VMEM((outer, rows, width), BF16),
            pltpu.VMEM((outer, rows, width), BF16),
            pltpu.VMEM((outer, rows, width), BF16),
            pltpu.VMEM((outer, rows, width), BF16),
            dma,
            dma((tensor,)),
            dma((tensor,)),
            dma((2, kv_count)),
            dma((4,)),
            dma((4, replicas)),
            dma((4, replicas)),
            dma((outer,)),
            dma((tensor,)),
            dma((outer,)),
            dma((2, tensor)),
            dma((2, tensor)),
            dma((outer,)),
            dma((outer,)),
            dma((outer,)),
            dma((outer,)),
        ],
        compiler_params=pltpu.CompilerParams(
            collective_id=0, has_side_effects=True, vmem_limit_bytes=58 * 1024 * 1024
        ),
    )(
        hidden,
        w_query,
        output_weight,
        keys,
        values,
        query_down,
        query_up,
        output_down,
        output_up,
        adapter_ids.reshape(1, -1),
        owner_map.reshape(1, -1),
        kv_lengths.reshape(1, -1),
    )


def solution(mesh):
    return jax.shard_map(
        functools.partial(per_device, mesh.shape["tensor"], mesh.shape["replica"]),
        mesh=mesh,
        in_specs=(
            P(("groups", "replica"), "tensor"),
            P(None, "tensor"),
            P("tensor", None),
            P(("groups", "replica"), None, None, None),
            P(("groups", "replica"), None, None, None),
            P(("groups", "replica"), None, "tensor"),
            P(("groups", "replica"), None, "tensor"),
            P(("groups", "replica"), None, "tensor"),
            P(("groups", "replica"), None, "tensor"),
            P("groups"),
            P("groups"),
            P(("groups", "replica")),
        ),
        out_specs=P(("groups", "replica"), "tensor"),
        check_vma=False,
    )
```

profile of v0, /device:TPU:0, one launch (start us, length us, event | category | flops | bytes accessed | tf_op | source)
XLA Modules:
  0.0 34.3 jit_solution(8315911292355587795)
XLA Ops:
  0.0 33.6 %shard_map.118 = bf16[32,1024]{1,0:T(8,128)(2,1)S(1)} custom-call(bf16[32,1024]{1,0:T(8,128)(2,1)} %hidden.1, bf16[8192,1024]{1,0:T(8,128)(2,1)} %w_query.1, bf16[1024,8192]{1,0:T(8,128)(2,1)} %output_weight.1, bf16[32,8,32,128]{3,2,1,0:T(8,128)(2,1)} %keys.1, bf16[32,8,32,128]{3,2,1,0:T(8,128)(2,1)} %values.1, bf16[4,64,1024]{2,1,0:T(8,128)(2,1)} %query_down.1, ...), custom_call_target="tpu_custom_call" | custom-call | tf_op jit(solution)/shard_map/pallas_call | solution.py:410
  33.6 0.6 %copy.14 = bf16[32,1024]{1,0:T(8,128)(2,1)} copy(bf16[32,1024]{1,0:T(8,128)(2,1)S(1)} %shard_map.118) | data formatting | bytes 131072
where the time goes:
time: 34.4 us; the launch traced here: 34.3 us
  Pallas kernels  33.6 us (98%)
  local copies, waits for them, and re-layouts  0.63 us (2%)
    pallas_call x1, Pallas kernels, per_device(): pl.pallas_call(functools.partial(block_kernel, tensor, replicas), out_sha...  33.6 us

commit v1 on v0

--- a/solution.py
+++ b/solution.py
@@ -150,15 +150,15 @@
     own_hidden.wait()
 
     h_sends = []
+    if inner == 2:
+        h_sends.append(
+            remote(h_buf.at[me], h_buf.at[me], h_send_sem.at[0], h_recv_sem.at[me], {"tensor": at(0, 1)})
+        )
     for k in range(1, outer):
         h_sends.append(
             remote(
                 h_buf.at[me], h_buf.at[me], h_send_sem.at[k], h_recv_sem.at[me], {"tensor": at(k, 0)}
             )
-        )
-    if inner == 2:
-        h_sends.append(
-            remote(h_buf.at[me], h_buf.at[me], h_send_sem.at[0], h_recv_sem.at[me], {"tensor": at(0, 1)})
         )
     for copy in h_sends:
         copy.start()
@@ -179,7 +179,6 @@
             map_copies[-1].start()
 
     send_map(0)
-    send_map(1)
     own_maps[1].start()
     for copy in kv_copies:
         copy.start()
@@ -282,6 +281,7 @@
 
     first, second = tensor * 3 // 8, tensor * 7 // 8
     loop(first, use_shard)
+    send_map(1)
     wait_map(0)
     low_copies = send_low(0, h_buf[me])
     loop(second, use_shard, first)
@@ -342,13 +342,6 @@
         pair_send[k] = product(at(k, 1)).astype(BF16)
         pair_copy(k).start()
 
-    early = outer // 2 if inner == 2 else 0
-    loop(early, to_pair)
-    wait_map(2)
-    low_copies += send_low(1, features)
-    if inner == 2:
-        loop(outer, to_pair, early)
-
     def own_sum(k):
         total = product(at(k, 0))
         if inner == 2:
@@ -360,7 +353,20 @@
         far_send[k] = own_sum(k).astype(BF16)
         far_copy(k).start()
 
-    loop(outer, to_far, 1)
+    early = min(2, outer) if inner == 2 else 0
+    loop(early, to_pair)
+    wait_map(2)
+    low_copies += send_low(1, features)
+
+    def both(n):
+        to_far(n - early + 1)
+        to_pair(n)
+
+    if inner == 2:
+        loop(outer, both, early)
+        loop(outer, to_far, outer - early + 1)
+    else:
+        loop(outer, to_far, 1)
     wait_map(3)
     total = adapter_delta(1)
     total = total + own_sum(0)

time: 34.4 us -> 34.4 us (level)
  no operation moved by 1% of the time
where the time goes in v1:
time: 34.4 us; the launch traced here: 34.2 us
  Pallas kernels  33.6 us (98%)
  local copies, waits for them, and re-layouts  0.63 us (2%)
    pallas_call x1, Pallas kernels, per_device(): pl.pallas_call(functools.partial(block_kernel, tensor, replicas), out_sha...  33.6 us

profile of v1, /device:TPU:0, one launch (start us, length us, event | category | flops | bytes accessed | tf_op | source)
XLA Modules:
  0.0 34.2 jit_solution(1629484414695546158)
XLA Ops:
  0.0 33.6 %shard_map.118 = bf16[32,1024]{1,0:T(8,128)(2,1)S(1)} custom-call(bf16[32,1024]{1,0:T(8,128)(2,1)} %hidden.1, bf16[8192,1024]{1,0:T(8,128)(2,1)} %w_query.1, bf16[1024,8192]{1,0:T(8,128)(2,1)} %output_weight.1, bf16[32,8,32,128]{3,2,1,0:T(8,128)(2,1)} %keys.1, bf16[32,8,32,128]{3,2,1,0:T(8,128)(2,1)} %values.1, bf16[4,64,1024]{2,1,0:T(8,128)(2,1)} %query_down.1, ...), custom_call_target="tpu_custom_call" | custom-call | tf_op jit(solution)/shard_map/pallas_call | solution.py:416
  33.6 0.6 %copy.14 = bf16[32,1024]{1,0:T(8,128)(2,1)} copy(bf16[32,1024]{1,0:T(8,128)(2,1)S(1)} %shard_map.118) | data formatting | bytes 131072

commit v2 on v1

--- a/solution.py
+++ b/solution.py
@@ -260,14 +260,10 @@
     def use_shard(n):
         following = shard(n + 1)
 
-        @pl.when(n + 1 < tensor)
+        @pl.when(n + 1 < outer)
         def _():
             wait_hidden(following)
-
-        if inner == 2:
-
-            @pl.when(n + 1 < outer)
-            def _():
+            if inner == 2:
                 forward(n + 1).start()
 
         @pl.when(n + ahead < tensor)
@@ -276,6 +272,11 @@
 
         ow_copy(target(n)).start()
         s = shard(n)
+
+        @pl.when(n >= outer)
+        def _():
+            wait_hidden(s)
+
         wq_copy(s).wait()
         acc[...] += jnp.dot(h_buf[s], wq_buf[s], preferred_element_type=F32)
 

time: 34.4 us -> 34.4 us (level)
  no operation moved by 1% of the time
where the time goes in v2:
time: 34.4 us; the launch traced here: 34.2 us
  Pallas kernels  33.6 us (98%)
  local copies, waits for them, and re-layouts  0.63 us (2%)
    pallas_call x1, Pallas kernels, per_device(): pl.pallas_call(functools.partial(block_kernel, tensor, replicas), out_sha...  33.6 us

profile of v2, /device:TPU:0, one launch (start us, length us, event | category | flops | bytes accessed | tf_op | source)
XLA Modules:
  0.0 34.2 jit_solution(8314146239153551756)
XLA Ops:
  0.0 33.6 %shard_map.118 = bf16[32,1024]{1,0:T(8,128)(2,1)S(1)} custom-call(bf16[32,1024]{1,0:T(8,128)(2,1)} %hidden.1, bf16[8192,1024]{1,0:T(8,128)(2,1)} %w_query.1, bf16[1024,8192]{1,0:T(8,128)(2,1)} %output_weight.1, bf16[32,8,32,128]{3,2,1,0:T(8,128)(2,1)} %keys.1, bf16[32,8,32,128]{3,2,1,0:T(8,128)(2,1)} %values.1, bf16[4,64,1024]{2,1,0:T(8,128)(2,1)} %query_down.1, ...), custom_call_target="tpu_custom_call" | custom-call | tf_op jit(solution)/shard_map/pallas_call | solution.py:417
  33.6 0.6 %copy.14 = bf16[32,1024]{1,0:T(8,128)(2,1)} copy(bf16[32,1024]{1,0:T(8,128)(2,1)S(1)} %shard_map.118) | data formatting | bytes 131072
